TPU v7x, 256 devices: a whole 4x4x8 slice. The times are simulated.
256 devices in a mesh: dp: 4 (over x), expert: 64 (over z, y, core).
Axes of the slice: x: 4, y: 4, z: 8, core: 2. Of those that a mesh axis runs over, the one named last changes fastest.
Arguments:
- query_nope: bfloat16 [64, 128, 2048], P('expert', None, 'dp'), may hold values from -6 to 6
- query_rope: bfloat16 [64, 128, 1024], P('expert', None, 'dp'), may hold values from -8 to 8
- latent_new: bfloat16 [64, 128, 512], P('expert'), may hold values from -6 to 6
- key_rope: bfloat16 [64, 128, 64], P('expert'), may hold values from -8 to 8
- latent_pages: bfloat16 [64, 16, 64, 512], P('expert', 'dp'), may hold values from -6 to 6
- rope_pages: bfloat16 [64, 16, 4096], P('expert', 'dp'), may hold values from -6 to 6
- page_table: int32 [64, 16], P('expert'), may hold values from 0 to 15, each once within a row
- prefix_lengths: int32 [64], P('expert'), may hold values from 0 to 1024, as said below
- residual: bfloat16 [64, 128, 2048], P('expert'), may hold values from -60 to 60
- key_up: bfloat16 [16, 128, 512], P('dp'), may hold values from -0.5 to 0.5
- value_up: bfloat16 [16, 512, 128], P('dp'), may hold values from -0.25 to 0.25
- out_weight: bfloat16 [2048, 2048], P('dp'), may hold values from -0.125 to 0.125
- norm_gain: float32 [2048], replicated, may hold values from 0.1 to 1.9
- expert_in: bfloat16 [64, 1408, 2, 2048], P('expert', 'dp'), may hold values from -0.125 to 0.125
- expert_down: bfloat16 [64, 1408, 2048], P('expert', 'dp'), may hold values from -0.15625 to 0.15625
- expert_ids: int32 [64, 128, 6], P('expert'), may hold values from 0 to 63, all different within a row; in each aligned block of 32 rows (0 to 31, 32 to 63, ..., all dimensions but the last counted through in order) at most 6 rows name the same one
- expert_weights: float32 [64, 128, 6], P('expert'), may hold values from 0.05 to 0.4
Outputs:
- layer_out: bfloat16 [64, 128, 2048], P('expert', 'dp')
- expert_mix: bfloat16 [64, 128, 2048], P('expert', 'dp')
Inputs may be any that keep to these rules, and one draw needn't show every extreme that they name: `prefix_lengths`: some request's prefix fills all of its 16 page slots. `page_table`: each row names every page slot of its request once; entry j holds positions j * 64 to (j + 1) * 64 - 1. `expert_ids`: each row names 6 distinct experts; in each aligned block of 32 rows of a request (blocks along the first two dimensions taken together) no expert is named more than 6 times, and that many is reached.
All inputs are finite; a program needn't handle non-finite values.
Results may differ from a plain program's by a relative error of at most 0.019.
Values may be sent and summed in bfloat16 or wider, within the bound.
No kernel may reach another device: no remote copies, remote signals or barrier semaphores. Data moves between devices by JAX's collectives and lax.ppermute only.
A program may use at most 128 MiB of HBM per device.

v0:
```python
import jax
import jax.numpy as jnp
from jax import lax
from jax.sharding import PartitionSpec as P

HD = 128
RD = 64
LAT = 512
TOP = 6
PAGE = 64


EPS = 1e-06
NEG = -1e30


def norm_rows(hidden, norm_gain):
    power = jnp.mean(hidden * hidden, axis=-1, keepdims=True)
    return (hidden * lax.rsqrt(power + EPS) * norm_gain).astype(jnp.bfloat16)


def expert_apply(tokens, expert_in, expert_down):
    flat = tokens.reshape(-1, tokens.shape[-1])
    dims = (((1,), (1,)), ((), ()))
    gate_act = lax.dot_general(
        flat, expert_in[0, :, 0, :], dims, preferred_element_type=jnp.float32
    )
    up_act = lax.dot_general(flat, expert_in[0, :, 1, :], dims, preferred_element_type=jnp.float32)
    units = (jax.nn.silu(gate_act) * up_act).astype(jnp.bfloat16)
    part = jnp.dot(units, expert_down[0], preferred_element_type=jnp.float32).astype(jnp.bfloat16)
    return part.reshape(tokens.shape)


def slot_table(ids, block_rows, block_offset, experts, stride):
    blocks = ids.reshape(-1, block_rows * TOP)
    onehot = (blocks[..., None] == jnp.arange(experts)[None, None, :]).astype(jnp.int32)
    before = jnp.cumsum(onehot, axis=1) - onehot
    rank = jnp.sum(before * onehot, axis=-1)
    offset = (jnp.arange(blocks.shape[0]) * block_offset)[:, None]
    return (blocks * stride + offset + rank).reshape(-1)


def pack_rows(tokens, slots, total):
    source = jnp.arange(slots.shape[0]) // TOP
    row_of = jnp.zeros((total,), jnp.int32).at[slots].set(source)
    filled = jnp.zeros((total,), jnp.bool_).at[slots].set(True)
    return jnp.where(filled[:, None], tokens[row_of], jnp.zeros((), tokens.dtype))


def combine(returned, slots, weights):
    values = returned.reshape(-1, returned.shape[-1])[slots]
    values = values.reshape(weights.shape[0], weights.shape[1], -1).astype(jnp.float32)
    return jnp.einsum("tk,tkd->td", weights, values)


def per_device(
    query_nope,
    query_rope,
    latent_new,
    key_rope,
    latent_pages,
    rope_pages,
    page_table,
    prefix_lengths,
    residual,
    key_up,
    value_up,
    out_weight,
    norm_gain,
    expert_in,
    expert_down,
    expert_ids,
    expert_weights,
):
    groups = lax.axis_size("dp")
    experts_all = lax.axis_size("expert") * expert_in.shape[0]
    tokens_col = query_nope.shape[1]
    block_rows = tokens_col // groups
    cap_block = min(block_rows, max(2, 2 * block_rows * TOP // experts_all))
    heads_here = key_up.shape[0]
    pages_lat, pages_rope = (
        lax.all_gather(latent_pages[0], "dp", axis=0, tiled=True),
        lax.all_gather(rope_pages[0], "dp", axis=0, tiled=True),
    )
    page_count = pages_lat.shape[0]
    table = page_table[0]
    inverse = jnp.sum(
        jnp.where(
            table[:, None] == jnp.arange(page_count)[None, :], jnp.arange(page_count)[:, None], 0
        ),
        axis=0,
    )
    positions = (inverse[:, None] * PAGE + jnp.arange(PAGE)[None, :]).reshape(-1)
    prefix_ok = positions < prefix_lengths[0]
    keys_lat = jnp.concatenate([pages_lat.reshape(-1, LAT), latent_new[0]], axis=0)
    keys_rope = jnp.concatenate([pages_rope.reshape(-1, RD), key_rope[0]], axis=0)
    heads_nope = query_nope[0].reshape(tokens_col, heads_here, HD)
    query_lat = jnp.einsum(
        "thd,hdc->thc", heads_nope, key_up, preferred_element_type=jnp.float32
    ).astype(jnp.bfloat16)
    heads_rope = query_rope[0].reshape(tokens_col, heads_here, RD)
    scale = 1.0 / (HD + RD) ** 0.5
    scores = (
        jnp.einsum("thc,kc->thk", query_lat, keys_lat, preferred_element_type=jnp.float32)
        + jnp.einsum("thr,kr->thk", heads_rope, keys_rope, preferred_element_type=jnp.float32)
    ) * scale
    causal = jnp.arange(tokens_col)[None, :] <= jnp.arange(tokens_col)[:, None]
    allowed = jnp.concatenate(
        [jnp.broadcast_to(prefix_ok[None, :], (tokens_col, prefix_ok.shape[0])), causal], axis=1
    )[:, None, :]
    masked = jnp.where(allowed, scores, NEG)
    peak = jnp.max(masked, axis=-1, keepdims=True)
    expo = jnp.where(allowed, jnp.exp(masked - peak), 0.0)
    total = jnp.sum(expo, axis=-1, keepdims=True)
    probs = expo.astype(jnp.bfloat16)
    attn_latent = (
        jnp.einsum("thk,kc->thc", probs, keys_lat, preferred_element_type=jnp.float32) / total
    ).astype(jnp.bfloat16)
    heads_out = jnp.einsum(
        "thc,hcd->thd", attn_latent, value_up, preferred_element_type=jnp.float32
    ).astype(jnp.bfloat16)
    partial_out = jnp.dot(
        heads_out.reshape(tokens_col, heads_here * HD),
        out_weight,
        preferred_element_type=jnp.float32,
    )
    attended = lax.psum(partial_out.astype(jnp.bfloat16), "dp").astype(jnp.float32)
    hidden = residual[0].astype(jnp.float32) + attended
    start = lax.axis_index("dp") * block_rows
    hidden_mine = lax.dynamic_slice_in_dim(hidden, start, block_rows, 0)
    normed = norm_rows(hidden, norm_gain)
    cap_column = cap_block * groups
    slots = slot_table(expert_ids[0], block_rows, cap_block, experts_all, cap_column)
    outgoing = pack_rows(normed, slots, experts_all * cap_column).reshape(
        experts_all, cap_column, -1
    )
    part = expert_apply(
        lax.all_to_all(outgoing, "expert", split_axis=0, concat_axis=0, tiled=True),
        expert_in,
        expert_down,
    )
    returned = lax.all_to_all(part, "expert", split_axis=0, concat_axis=0, tiled=True)
    mixed_column = combine(returned, slots, expert_weights[0])
    mixture = lax.psum_scatter(
        mixed_column.astype(jnp.bfloat16), "dp", scatter_dimension=0, tiled=True
    ).astype(jnp.float32)
    layer_out = (hidden_mine + mixture).astype(jnp.bfloat16)[None]
    return (layer_out, mixture.astype(jnp.bfloat16)[None])


def solution(mesh):
    return jax.shard_map(
        per_device,
        mesh=mesh,
        in_specs=(
            P("expert", None, "dp"),
            P("expert", None, "dp"),
            P("expert", None, None),
            P("expert", None, None),
            P("expert", "dp", None, None),
            P("expert", "dp", None),
            P("expert", None),
            P("expert"),
            P("expert", None, None),
            P("dp", None, None),
            P("dp", None, None),
            P("dp", None),
            P(),
            P("expert", "dp", None, None),
            P("expert", "dp", None),
            P("expert", None, None),
            P("expert", None, None),
        ),
        out_specs=(P("expert", "dp", None), P("expert", "dp", None)),
        check_vma=False,
    )
```

profile of v0, /device:TPU:1, one launch (start us, length us, event | category | flops | bytes accessed | tf_op | source)
XLA Modules:
  0.0 481.4 jit_solution(14480549456266452632)
XLA Ops:
  7.2 0.7 all-gather.4.cloned.1.call-update
  8.0 0.8 copy.55
  8.8 0.7 select_reduce_fusion
  10.2 0.8 copy.61
  11.0 0.1 eq.41
  11.2 2.4 reduce-window.6
  13.6 0.1 slice.24
  13.7 0.1 copy.63
  13.9 0.1 add_compare_fusion
  13.9 11.0 %all-gather.1 = bf16[1,16,4096]{2,0,1:T(2,128)(2,1)S(1)} all-gather(bf16[1,4,4096]{2,0,1:T(2,128)(2,1)S(1)} %copy.55), channel_id=3, replica_groups=mesh['dp'=4,'expert'=64] {'dp'}, dimensions={1}, use_global_device_ids=true | all-gather | bytes 163840 | tf_op jit(solution)/shard_map/all_gather | solution.py:83
  24.9 0.7 reduce
  25.7 0.2 reshape.130
  25.9 0.1 copy.56
  26.1 0.1 copy.57
  26.2 0.1 reshape.184
  26.3 0.1 bitcast_bitcast_fusion
  26.6 0.1 reduce_sum.41
  26.6 0.1 copy.60
  26.8 0.1 mul.76
  27.0 0.1 add.105
  27.1 1.9 convolution_bitcast_fusion
  29.1 10.2 %all-gather.4.cloned.1.call-done = bf16[1,16,64,512]{3,2,0,1:T(8,128)(2,1)} async-done(((bf16[1,4,64,512]{3,2,0,1:T(8,128)(2,1)}), bf16[1,16,64,512]{3,2,0,1:T(8,128)(2,1)}) %all-gather.4.cloned.1.call-update) | async-done | bytes 1048592 | tf_op jit(solution)/shard_map/all_gather | solution.py:82
  39.3 4.9 %fusion.42 = (f32[128,4]{0,1:T(4,128)S(1)}, bf16[128,4,1152]{2,0,1:T(8,128)(2,1)}) fusion(pred[128,1152]{1,0:T(8,128)(4,1)S(1)} %pad_add_fusion, f32[128,4,1152]{2,0,1:T(8,128)} %convolution_bitcast_fusion, bf16[4,128,512]{2,1,0:T(8,128)(2,1)S(1)} %copy-done.11, bf16[128,512]{1,0:T(8,128)(2,1)S(1)} %bitcast.94, bf16[1024,512]{1,0:T(8,128)(2,1)} %bitcast.92, ...), kind=kOutput, calls=%fused_computation.81 | convolution fusion | flops 677840000 | bytes 5523456 | tf_op jit(solution)/shard_map/sub | solution.py:113
  44.2 2.7 fusion.15
  47.0 1.3 convolution_convert_fusion.1
  48.3 3.4 scatter_custom_fusion.1
  51.7 3.6 scatter_custom_fusion
  55.3 0.1 broadcast_in_dim.90
  55.4 40.6 %all-reduce.3.cloned.1.call-done = bf16[128,2048]{1,0:T(8,128)(2,1)} async-done(((bf16[128,2048]{1,0:T(8,128)(2,1)}), bf16[128,2048]{1,0:T(8,128)(2,1)}) %all-reduce.3.cloned.1.call-update) | async-done | bytes 524304 | tf_op jit(solution)/shard_map/psum | solution.py:127
  96.0 2.3 convert_add_fusion
  98.3 0.2 multiply_convert_fusion
  98.5 7.1 %gather_fusion = bf16[1536,2048]{1,0:T(8,128)(2,1)} fusion(bf16[128,2048]{1,0:T(8,128)(2,1)S(1)} %multiply_convert_fusion, s32[2048]{0:T(1024)S(1)} %pad_clamp_fusion), kind=kCustom, calls=%fused_computation | custom fusion | bytes 12589056 | tf_op jit(solution)/shard_map/gather | solution.py:47
  105.6 5.9 %broadcast_select_fusion = bf16[64,24,2048]{2,1,0:T(8,128)(2,1)} fusion(bf16[64,24,2048]{2,1,0:T(8,128)(2,1)} %bitcast.83, pred[64,24]{1,0:T(8,128)(4,1)S(1)} %broadcast_in_dim.90), kind=kLoop, calls=%fused_computation.6 | loop fusion | flops 3145728 | bytes 12584448 | tf_op jit(solution)/shard_map/jit(_where)/select_n | solution.py:47
  111.5 12.7 %all-to-all-start = ((bf16[64,24,2048]{2,1,0:T(8,128)(2,1)}), bf16[64,24,2048]{2,1,0:T(8,128)(2,1)}, u32[]{:S(2)}, u32[]{:S(2)}) async-start(bf16[64,24,2048]{2,1,0:T(8,128)(2,1)} %broadcast_select_fusion), calls=%async_computation | async-start | bytes 12582912 | tf_op jit(solution)/shard_map/all_to_all | solution.py:138
  124.2 8.9 %fusion.41 = (bf16[1,352,1,2048]{3,2,1,0:T(2,128)(2,1)}, bf16[1,352,1,2048]{3,2,1,0:T(2,128)(2,1)}) fusion(bf16[1,352,2,2048]{3,2,1,0:T(2,128)(2,1)} %param.30), kind=kLoop, calls=%fused_computation.80 | loop fusion | bytes 5767168 | tf_op jit(solution)/shard_map/slice | solution.py:28
  133.2 129.6 %all-to-all-done = bf16[64,24,2048]{2,1,0:T(8,128)(2,1)} async-done(((bf16[64,24,2048]{2,1,0:T(8,128)(2,1)}), bf16[64,24,2048]{2,1,0:T(8,128)(2,1)}, u32[]{:S(2)}, u32[]{:S(2)}) %all-to-all-start) | async-done | bytes 6291488 | tf_op jit(solution)/shard_map/all_to_all | solution.py:138
  262.7 7.8 %fusion.7 = f32[1536,352]{0,1:T(8,128)} fusion(bf16[1536,2048]{1,0:T(8,128)(2,1)} %bitcast.17, bf16[1,352,1,2048]{3,2,1,0:T(2,128)(2,1)} %get-tuple-element.3), kind=kOutput, calls=%fused_computation.19 | convolution fusion | flops 2214592512 | bytes 9895936 | tf_op jit(solution)/shard_map/dot_general | solution.py:25
  270.6 13.0 %convolution_convert_fusion = bf16[1536,2048]{1,0:T(8,128)(2,1)} fusion(bf16[1,352,2048]{2,1,0:T(8,128)(2,1)S(1)} %copy-done.10, bf16[1536,2048]{1,0:T(8,128)(2,1)} %bitcast.17, f32[1536,352]{0,1:T(8,128)} %fusion.7, bf16[1,352,1,2048]{3,2,1,0:T(2,128)(2,1)} %get-tuple-element.2), kind=kOutput, calls=%fused_computation.5 | convolution fusion | flops 4435574784 | bytes 17629184 | tf_op jit(solution)/shard_map/dot_general | solution.py:30
  283.6 8.6 %all-to-all-start.1 = ((bf16[64,24,2048]{2,1,0:T(8,128)(2,1)}), bf16[64,24,2048]{2,1,0:T(8,128)(2,1)}, u32[]{:S(2)}, u32[]{:S(2)}) async-start(bf16[64,24,2048]{2,1,0:T(8,128)(2,1)} %bitcast.84), calls=%async_computation.1 | async-start | bytes 12582912 | tf_op jit(solution)/shard_map/all_to_all | solution.py:142
  292.2 0.3 reduce-scatter.2.cloned.1.call-start
  292.5 0.1 copy.74
  292.6 138.1 %all-to-all-done.1 = bf16[64,24,2048]{2,1,0:T(8,128)(2,1)} async-done(((bf16[64,24,2048]{2,1,0:T(8,128)(2,1)}), bf16[64,24,2048]{2,1,0:T(8,128)(2,1)}, u32[]{:S(2)}, u32[]{:S(2)}) %all-to-all-start.1) | async-done | bytes 6291488 | tf_op jit(solution)/shard_map/all_to_all | solution.py:142
  430.8 10.8 %gather_fusion.1 = bf16[768,2048]{1,0:T(8,128)(2,1)} fusion(bf16[1536,2048]{1,0:T(8,128)(2,1)} %bitcast.22, s32[1024]{0:T(1024)S(1)} %pad_clamp_fusion.1), kind=kCustom, calls=%fused_computation.1 | custom fusion | bytes 6294528 | tf_op jit(solution)/shard_map/gather | solution.py:51
  441.5 6.3 %reshape.137 = bf16[128,6,2048]{2,1,0:T(8,128)(2,1)} reshape(bf16[768,2048]{1,0:T(8,128)(2,1)} %gather_fusion.1) | data formatting | bytes 6291456 | tf_op jit(solution)/shard_map/reshape | solution.py:52
  447.8 3.6 fusion.45
  451.4 1.1 copy.93
  452.5 20.7 %reduce-scatter.2.cloned.1.call-done = bf16[32,2048]{1,0:T(8,128)(2,1)} async-done(((bf16[128,2048]{1,0:T(8,128)(2,1)}), bf16[32,2048]{1,0:T(8,128)(2,1)}) %reduce-scatter.2.cloned.1.call-update) | async-done | bytes 131088 | tf_op jit(solution)/shard_map/reduce_scatter | solution.py:144
  473.2 1.7 fusion.23
  (51 shorter events, 0.6 us)
Async XLA Ops:
  7.2 39.8 %copy-start = (bf16[512,2048]{1,0:T(8,128)(2,1)S(1)}, bf16[512,2048]{1,0:T(8,128)(2,1)}, u32[]{:S(2)}) copy-start(bf16[512,2048]{1,0:T(8,128)(2,1)} %param.28) | copy-start | bytes 6291460
  7.2 18.9 %copy-start.5 = (bf16[1,128,256]{2,1,0:T(8,128)(2,1)S(1)}, bf16[1,128,256]{2,1,0:T(8,128)(2,1)}, u32[]{:S(2)}) copy-start(bf16[1,128,256]{2,1,0:T(8,128)(2,1)} %param.18) | copy-start | bytes 196612
  7.2 19.1 %copy-start.4 = (bf16[1,128,512]{2,1,0:T(8,128)(2,1)S(1)}, bf16[1,128,512]{2,1,0:T(8,128)(2,1)}, u32[]{:S(2)}) copy-start(bf16[1,128,512]{2,1,0:T(8,128)(2,1)} %param.17) | copy-start | bytes 393220
  7.2 32.1 %all-gather.4.cloned.1.call-start = ((), (), s32[]{:S(2)}) async-start(), calls=%async_computation.5 | async-start | bytes 1310720 | tf_op jit(solution)/shard_map/all_gather | solution.py:82
  7.9 18.7 %copy-start.7 = (s32[1,128,6]{1,0,2:T(1,128)S(1)}, s32[1,128,6]{1,0,2:T(1,128)}, u32[]{:S(2)}) copy-start(s32[1,128,6]{1,0,2:T(1,128)} %param.32) | copy-start | bytes 9220
  7.9 88.0 %all-reduce.3.cloned.1.call-start = ((), (), s32[]{:S(2)}) async-start(), calls=%async_computation.3 | async-start | bytes 1048576 | tf_op jit(solution)/shard_map/psum | solution.py:127
  11.0 16.1 %copy-start.6 = (bf16[1,128,64]{1,2,0:T(8,128)(2,1)S(1)}, bf16[1,128,64]{1,2,0:T(8,128)(2,1)}, u32[]{:S(2)}) copy-start(bf16[1,128,64]{1,2,0:T(8,128)(2,1)} %param.20) | copy-start | bytes 49156
  25.9 13.4 %copy-start.11 = (bf16[4,128,512]{2,1,0:T(8,128)(2,1)S(1)}, bf16[4,128,512]{2,1,0:T(8,128)(2,1)}, u32[]{:S(2)}) copy-start(bf16[4,128,512]{2,1,0:T(8,128)(2,1)} %param.26) | copy-start | bytes 1572868
  27.1 12.2 %copy-start.12 = (bf16[1,128,512]{2,1,0:T(8,128)(2,1)S(1)}, bf16[1,128,512]{2,1,0:T(8,128)(2,1)}, u32[]{:S(2)}) copy-start(bf16[1,128,512]{2,1,0:T(8,128)(2,1)} %param.19) | copy-start | bytes 393220
  46.9 49.0 %copy-start.2 = (bf16[1,128,2048]{2,1,0:T(8,128)(2,1)S(1)}, bf16[1,128,2048]{2,1,0:T(8,128)(2,1)}, u32[]{:S(2)}) copy-start(bf16[1,128,2048]{2,1,0:T(8,128)(2,1)} %param.25) | copy-start | bytes 1572868
  47.0 51.3 %copy-start.8 = (f32[2048]{0:T(1024)S(1)}, f32[2048]{0:T(1024)}, u32[]{:S(2)}) copy-start(f32[2048]{0:T(1024)} %param.29) | copy-start | bytes 24580
  96.0 2.3 copy-start.3
  111.5 151.2 %all-to-all-start = ((bf16[64,24,2048]{2,1,0:T(8,128)(2,1)}), bf16[64,24,2048]{2,1,0:T(8,128)(2,1)}, u32[]{:S(2)}, u32[]{:S(2)}) async-start(bf16[64,24,2048]{2,1,0:T(8,128)(2,1)} %broadcast_select_fusion), calls=%async_computation | async-start | bytes 12582912 | tf_op jit(solution)/shard_map/all_to_all | solution.py:138
  262.7 7.8 %copy-start.10 = (bf16[1,352,2048]{2,1,0:T(8,128)(2,1)S(1)}, bf16[1,352,2048]{2,1,0:T(8,128)(2,1)}, u32[]{:S(2)}) copy-start(bf16[1,352,2048]{2,1,0:T(8,128)(2,1)} %param.31) | copy-start | bytes 4325380
  283.6 8.9 %copy-start.9 = (f32[1,128,6]{1,0,2:T(1,128)S(1)}, f32[1,128,6]{1,0,2:T(1,128)}, u32[]{:S(2)}) copy-start(f32[1,128,6]{1,0,2:T(1,128)} %param.33) | copy-start | bytes 9220
  283.6 147.1 %all-to-all-start.1 = ((bf16[64,24,2048]{2,1,0:T(8,128)(2,1)}), bf16[64,24,2048]{2,1,0:T(8,128)(2,1)}, u32[]{:S(2)}, u32[]{:S(2)}) async-start(bf16[64,24,2048]{2,1,0:T(8,128)(2,1)} %bitcast.84), calls=%async_computation.1 | async-start | bytes 12582912 | tf_op jit(solution)/shard_map/all_to_all | solution.py:142
  292.2 181.0 %reduce-scatter.2.cloned.1.call-start = ((), (), s32[]{:S(2)}) async-start(), calls=%async_computation.4 | async-start | bytes 655360 | tf_op jit(solution)/shard_map/reduce_scatter | solution.py:144
  447.8 27.1 %copy-start.1 = (bf16[512,2048]{1,0:T(8,128)(2,1)S(1)}, bf16[512,2048]{1,0:T(8,128)(2,1)}, u32[]{:S(2)}) copy-start(bf16[512,2048]{1,0:T(8,128)(2,1)} %param.28) | copy-start | bytes 6291460
Sparse Core Ops, SparseCore 0:
  9.8 29.3 all-gather.3
  48.4 47.5 all-reduce.2
  452.6 20.5 reduce-scatter.1
where the time goes:
time: 483 us; the launch traced here: 481 us
  waiting for transfers between devices  340 us (70%)
  local copies, waits for them, and re-layouts  44.5 us (9%)
  matrix products  35.3 us (7%)
  starting transfers between devices  21.6 us (4%)
  between operations  14.7 us (3%)
  other arithmetic  14.5 us (3%)
  blocking collectives  11 us (2%)
    all_to_all x1, waiting for transfers between devices, per_device(): lax.all_to_all(part, 'expert', split_axis=0, concat_axis=0, tiled=True)  138 us
    all_to_all x1, waiting for transfers between devices, per_device(): lax.all_to_all(outgoing, 'expert', split_axis=0, concat_axis=0, tiled=True)  130 us
    psum x1, waiting for transfers between devices, per_device(): lax.psum(partial_out.astype(jnp.bfloat16), 'dp').astype(jnp.float32)  40.6 us
    reduce_scatter x1, waiting for transfers between devices, per_device(): lax.psum_scatter(mixed_column.astype(jnp.bfloat16), 'dp', scatter_dimensi...  20.7 us
    dot_general x1, matrix products, expert_apply(): jnp.dot(units, expert_down[0], preferred_element_type=jnp.float32)  13 us
    all_to_all x1, starting transfers between devices, per_device(): lax.all_to_all(outgoing, 'expert', split_axis=0, concat_axis=0, tiled=True)  12.7 us
    all_gather x1, blocking collectives, per_device(): lax.all_gather(rope_pages[0], 'dp', axis=0, tiled=True)  11 us
    gather x1, local copies, waits for them, and re-layouts, combine(): values = returned.reshape(-1, returned.shape[-1])[slots]  10.8 us
  transfers between devices with their start and end apart: 5, of which 5 were waited for; matrix products, arithmetic and copies ran while one was open for 5% of the time, Pallas kernels for 0%

commit v1 on v0

v1 whole, which is shorter than its diff:
```python
import functools

import jax
import jax.numpy as jnp
from jax import lax
from jax.experimental import pallas as pl
from jax.experimental.pallas import tpu as pltpu
from jax.sharding import PartitionSpec as P

HD = 128
RD = 64
LAT = 512
TOP = 6
PAGE = 64
EPS = 1e-06
NEG = -1e30

QUARTERS = 4
PAIR = 2
TILE = QUARTERS * PAIR
BLOCK = 256
BF = jnp.bfloat16
F32 = jnp.float32


def mm(a, b):
    return jnp.dot(a, b, preferred_element_type=F32)


def mm_nt(a, b):
    return lax.dot_general(a, b, (((1,), (1,)), ((), ())), preferred_element_type=F32)


def mm_tn(a, b):
    return lax.dot_general(a, b, (((0,), (0,)), ((), ())), preferred_element_type=F32)


def vmem(n):
    return [pl.BlockSpec(memory_space=pltpu.VMEM) for _ in range(n)]


def params(mib):
    return pltpu.CompilerParams(vmem_limit_bytes=mib * 2**20)


def attend_kernel(qn, qr, ku, k0, k1, k2, k3, kn, bias, vu, ow, out, q_scr, ho_scr):
    tokens = qn.shape[0]
    heads = ku.shape[0]
    width = q_scr.shape[1]
    for h in range(heads):
        rows = pl.ds(h * tokens, tokens)
        q_scr[rows, 0:LAT] = mm(qn[:, h * HD : (h + 1) * HD], ku[h]).astype(BF)
        rope = qr[:, h * RD : (h + 1) * RD]
        q_scr[rows, LAT:width] = jnp.concatenate(
            [rope, jnp.zeros((tokens, width - LAT - RD), BF)], axis=1
        )
    scale = 1.0 / (HD + RD) ** 0.5
    keys = (k0, k1, k2, k3)
    span = k0.shape[0]
    step = 2
    for h0 in range(0, heads, step):
        n = step * tokens
        q = q_scr[pl.ds(h0 * tokens, n), :]
        row = lax.rem(lax.broadcasted_iota(jnp.int32, (n, tokens), 0), tokens)
        col = lax.broadcasted_iota(jnp.int32, (n, tokens), 1)
        s_new = jnp.where(col <= row, mm_nt(q, kn[...]) * scale, NEG)
        s_old = [
            mm_nt(q, k[...]) * scale + bias[:, i * span : (i + 1) * span]
            for i, k in enumerate(keys)
        ]
        peak = jnp.max(s_new, axis=1, keepdims=True)
        for s in s_old:
            peak = jnp.maximum(peak, jnp.max(s, axis=1, keepdims=True))
        e = jnp.exp(s_new - peak)
        total = jnp.sum(e, axis=1, keepdims=True)
        acc = mm(e.astype(BF), kn[:, 0:LAT])
        for s, k in zip(s_old, keys):
            e = jnp.exp(s - peak)
            total = total + jnp.sum(e, axis=1, keepdims=True)
            acc = acc + mm(e.astype(BF), k[:, 0:LAT])
        latent = (acc / total).astype(BF)
        for i in range(step):
            ho_scr[:, (h0 + i) * HD : (h0 + i + 1) * HD] = mm(
                latent[i * tokens : (i + 1) * tokens], vu[h0 + i]
            ).astype(BF)
    for c in range(0, out.shape[1], 512):
        out[:, c : c + 512] = mm(ho_scr[...], ow[:, c : c + 512]).astype(BF)


def route_kernel(ids, gates, pick, high, low):
    experts = pick.shape[1] // TILE
    lanes = ids.shape[1]
    block = lanes // QUARTERS
    expert = lax.broadcasted_iota(jnp.int32, (experts, lanes), 0)
    named = jnp.zeros((experts, lanes), F32)
    gate = jnp.zeros((experts, lanes), F32)
    for k in range(TOP):
        hit = (ids[k : k + 1, :] == expert).astype(F32)
        named = named + hit
        gate = gate + hit * gates[k : k + 1, :]
    a = lax.broadcasted_iota(jnp.int32, (lanes, lanes), 0)
    b = lax.broadcasted_iota(jnp.int32, (lanes, lanes), 1)
    earlier = ((a // block == b // block) & (a < b)).astype(BF)
    rank = mm(named.astype(BF), earlier)
    rank = jnp.where(named > 0, rank, -1.0).astype(BF)
    gate_high = gate.astype(BF)
    gate_low = (gate - gate_high.astype(F32)).astype(BF)
    total = experts * TILE
    r = lax.broadcasted_iota(jnp.int32, (total, experts), 0)
    c = lax.broadcasted_iota(jnp.int32, (total, experts), 1)
    spread = (r // TILE == c).astype(BF)
    rank_r = mm(spread, rank)
    high_r = mm(spread, gate_high)
    low_r = mm(spread, gate_low)
    row = lax.broadcasted_iota(jnp.int32, (total, lanes), 0)
    lane = lax.broadcasted_iota(jnp.int32, (total, lanes), 1)
    same = lax.rem(row, TILE) // PAIR == lane // block
    slot = lax.rem(row, PAIR)
    for i in range(pick.shape[0]):
        on = same & (rank_r == (slot + i * PAIR).astype(F32))
        pick[i] = jnp.where(on, 1.0, 0.0).astype(BF)
        high[i] = jnp.where(on, high_r, 0.0).astype(BF)
        low[i] = jnp.where(on, low_r, 0.0).astype(BF)


def pack_kernel(partial, residual, gain, pick, hidden_out, *outgoing):
    hidden = residual[...].astype(F32)
    attended = partial[0].astype(F32)
    for i in range(1, partial.shape[0]):
        attended = attended + partial[i].astype(F32)
    hidden = hidden + attended
    hidden_out[...] = hidden
    power = jnp.mean(hidden * hidden, axis=1, keepdims=True)
    normed = (hidden * lax.rsqrt(power + EPS) * gain[...]).astype(BF)
    w = normed.shape[1] // QUARTERS
    stacked = jnp.concatenate([normed[:, q * w : (q + 1) * w] for q in range(QUARTERS)], axis=0)
    for i, out in enumerate(outgoing):
        out[...] = mm(pick[i], stacked).astype(BF)


def reorder(transposed):
    i = lax.broadcasted_iota(jnp.int32, (BLOCK, BLOCK), 1 if transposed else 0)
    j = lax.broadcasted_iota(jnp.int32, (BLOCK, BLOCK), 0 if transposed else 1)
    group = BLOCK // QUARTERS
    rest = lax.rem(i, group)
    source = (rest // PAIR) * TILE + (i // group) * PAIR + lax.rem(rest, PAIR)
    return (j == source).astype(BF)


def hidden_units(x, w):
    n = w.shape[0] // 3
    gate = mm_nt(x, w[0:n, :])
    up = mm_nt(x, w[n : 2 * n, :])
    return (gate / (1.0 + jnp.exp(-gate)) * up).astype(BF)


def expert_kernel(x0, xl, xr, wa, wb, ra, rb, y0, yl, yr, rows, acc):
    n = wa.shape[0] // 3
    there = reorder(False)
    back = reorder(True)
    group = BLOCK // QUARTERS
    w = x0.shape[1]
    blocks = x0.shape[0] // BLOCK
    each = blocks * group
    for i, x in enumerate((x0, xl, xr)):
        for b in range(blocks):
            sorted_rows = mm(there, x[b * BLOCK : (b + 1) * BLOCK, :]).astype(BF)
            for q in range(QUARTERS):
                rows[pl.ds(i * each + b * group, group), q * w : (q + 1) * w] = sorted_rows[
                    q * group : (q + 1) * group
                ]
    ua = hidden_units(rows[...], wa)
    ub = hidden_units(rows[...], wb)
    acc[...] = mm(ua, wa[2 * n : 3 * n, :]) + mm(ub, wb[2 * n : 3 * n, :])
    for i, extra in ((1, ra), (2, rb)):
        part = pl.ds(i * each, each)
        u = hidden_units(rows[part, :], extra)
        acc[part, :] += mm(u, extra[2 * n : 3 * n, :])
    for i, y in enumerate((y0, yl, yr)):
        for b in range(blocks):
            part = acc[pl.ds(i * each + b * group, group), :].astype(BF)
            stacked = jnp.concatenate(
                [part[:, q * w : (q + 1) * w] for q in range(QUARTERS)], axis=0
            )
            y[b * BLOCK : (b + 1) * BLOCK, :] = mm(back, stacked).astype(BF)


def combine_kernel(hidden, high, low, *rest):
    returned, (layer_out, mix_out) = rest[:-2], rest[-2:]
    mixed = None
    for i, r in enumerate(returned):
        term = mm_tn(high[i], r[...]) + mm_tn(low[i], r[...])
        mixed = term if mixed is None else mixed + term
    block = mixed.shape[0] // QUARTERS
    w = mixed.shape[1]
    for q in range(QUARTERS):
        part = mixed[q * block : (q + 1) * block]
        cols = slice(q * w, (q + 1) * w)
        mix_out[:, cols] = part.astype(BF)
        layer_out[:, cols] = (hidden[:, cols] + part).astype(BF)


def per_device(
    query_nope,
    query_rope,
    latent_new,
    key_rope,
    latent_pages,
    rope_pages,
    page_table,
    prefix_lengths,
    residual,
    key_up,
    value_up,
    out_weight,
    norm_gain,
    expert_in,
    expert_down,
    expert_ids,
    expert_weights,
):
    groups = lax.axis_size("dp")
    experts = lax.axis_size("expert")
    me = lax.axis_index("dp")
    tokens, width = residual.shape[1:]
    block = tokens // groups
    pages_here = latent_pages.shape[1]
    span = pages_here * PAGE
    pages = pages_here * groups
    chunks = 3
    rows = experts * TILE
    quarter = width // QUARTERS
    shape = jax.ShapeDtypeStruct

    def shift(x, k):
        return lax.ppermute(x, "dp", [(i, (i + k) % groups) for i in range(groups)])

    pad = LAT // 4 - RD
    keys = jnp.concatenate(
        [
            latent_pages[0].reshape(span, LAT),
            rope_pages[0].reshape(span, RD),
            jnp.zeros((span, pad), BF),
        ],
        axis=1,
    )
    keys_new = jnp.concatenate([latent_new[0], key_rope[0], jnp.zeros((tokens, pad), BF)], axis=1)
    from_left, from_right, from_far = shift(keys, 1), shift(keys, -1), shift(keys, 2)

    holders = lax.rem(me + jnp.array([0, 3, 1, 2], jnp.int32), groups)
    slot = (holders[:, None] * pages_here + jnp.arange(pages_here)[None, :]).reshape(-1)
    place = jnp.sum(
        jnp.where(page_table[0][None, :] == slot[:, None], jnp.arange(pages)[None, :], 0), axis=1
    )
    position = place[:, None] * PAGE + jnp.arange(PAGE)[None, :]
    bias = jnp.where(position < prefix_lengths[0], 0.0, NEG).astype(F32).reshape(1, span * groups)

    start = me * block
    ids = lax.dynamic_slice_in_dim(expert_ids[0], start, block, 0)
    gates = lax.dynamic_slice_in_dim(expert_weights[0], start, block, 0)
    residual_mine = lax.dynamic_slice_in_dim(residual[0], start, block, 0)
    lanes = block * QUARTERS
    pick, high, low = pl.pallas_call(
        route_kernel,
        out_shape=[shape((chunks, rows, lanes), BF)] * 3,
        in_specs=vmem(2),
        out_specs=vmem(3),
        compiler_params=params(32),
        name="route",
    )(jnp.tile(ids.T, (1, QUARTERS)), jnp.tile(gates.T, (1, QUARTERS)))

    half = expert_in.shape[1] // 2

    def half_weights(i):
        part = slice(i * half, (i + 1) * half)
        return jnp.concatenate(
            [expert_in[0, part, 0, :], expert_in[0, part, 1, :], expert_down[0, part, :]], axis=0
        )

    wa, wb = half_weights(0), half_weights(1)
    ra, rb = shift(wa, -1), shift(wb, 1)

    partial = pl.pallas_call(
        attend_kernel,
        out_shape=shape((tokens, width), BF),
        in_specs=vmem(11),
        out_specs=vmem(1)[0],
        scratch_shapes=[
            pltpu.VMEM((key_up.shape[0] * tokens, keys.shape[1]), BF),
            pltpu.VMEM((tokens, key_up.shape[0] * HD), BF),
        ],
        compiler_params=params(48),
        name="attend",
    )(
        query_nope[0],
        query_rope[0],
        key_up,
        keys,
        from_left,
        from_right,
        from_far,
        keys_new,
        bias,
        value_up,
        out_weight,
    )
    partial = lax.all_to_all(
        partial.reshape(groups, block, width), "dp", split_axis=0, concat_axis=0, tiled=True
    )
    hidden, *outgoing = pl.pallas_call(
        pack_kernel,
        out_shape=[shape((block, width), F32)] + [shape((rows, quarter), BF)] * chunks,
        in_specs=vmem(4),
        out_specs=vmem(1 + chunks),
        compiler_params=params(32),
        name="pack",
    )(partial, residual_mine, norm_gain.reshape(1, width), pick)

    def swap(x):
        x = x.reshape(experts, TILE, quarter)
        x = lax.all_to_all(x, "expert", split_axis=0, concat_axis=0, tiled=True)
        return x.reshape(rows, quarter)

    each = rows // QUARTERS
    expert_call = pl.pallas_call(
        expert_kernel,
        out_shape=[shape((rows, quarter), BF)] * 3,
        in_specs=vmem(7),
        out_specs=vmem(3),
        scratch_shapes=[pltpu.VMEM((3 * each, width), BF), pltpu.VMEM((3 * each, width), F32)],
        compiler_params=params(48),
        name="experts",
    )
    arrived = [swap(x) for x in outgoing]
    returned = []
    for x in arrived:
        own, left, right = expert_call(x, shift(x, 1), shift(x, -1), wa, wb, ra, rb)
        total = own.astype(F32) + shift(left, -1).astype(F32) + shift(right, 1).astype(F32)
        returned.append(swap(total.astype(BF)))

    layer_out, mix = pl.pallas_call(
        combine_kernel,
        out_shape=[shape((block, width), BF)] * 2,
        in_specs=vmem(3 + chunks),
        out_specs=vmem(2),
        compiler_params=params(32),
        name="combine",
    )(hidden, high, low, *returned)
    return layer_out[None], mix[None]


def solution(mesh):
    return jax.shard_map(
        per_device,
        mesh=mesh,
        in_specs=(
            P("expert", None, "dp"),
            P("expert", None, "dp"),
            P("expert", None, None),
            P("expert", None, None),
            P("expert", "dp", None, None),
            P("expert", "dp", None),
            P("expert", None),
            P("expert"),
            P("expert", None, None),
            P("dp", None, None),
            P("dp", None, None),
            P("dp", None),
            P(),
            P("expert", "dp", None, None),
            P("expert", "dp", None),
            P("expert", None, None),
            P("expert", None, None),
        ),
        out_specs=(P("expert", "dp", None), P("expert", "dp", None)),
        check_vma=False,
    )
```

time: 483 us -> 297 us (0.61)
  waiting for transfers between devices: 340 us -> 96.9 us
  starting transfers between devices: 21.6 us -> 93 us
  matrix products: 35.3 us -> 0 us
  Pallas kernels: 0 us -> 34.3 us
  blocking collectives: 11 us -> 28.5 us
  local copies, waits for them, and re-layouts: 44.5 us -> 29.8 us
  between operations: 14.7 us -> 1.82 us
  other arithmetic: 14.5 us -> 8.05 us
    all_to_all x2 -> x6, waiting for transfers between devices: 268 us -> 48.9 us  [the longest x1 24.5 us: per_device(): lax.all_to_all(partial.reshape(groups, block, width), 'dp', split_axis=0,...]
    ppermute x0 -> x17, waiting for transfers between devices: none -> 48 us  [shift(): return lax.ppermute(x, 'dp', [(i, (i + k) % groups) for i in range(groups)])]
    all_to_all x2 -> x6, starting transfers between devices: 21.3 us -> 64.8 us  [the longest x5 61.3 us: swap(): x = lax.all_to_all(x, 'expert', split_axis=0, concat_axis=0, tiled=True)]
    psum x1 -> x0, waiting for transfers between devices: 40.6 us -> none  [per_device(): lax.psum(partial_out.astype(jnp.bfloat16), 'dp').astype(jnp.float32)]
    pallas_call x0 -> x7, Pallas kernels: none -> 34.3 us  [the longest x3 24.6 us: per_device(): own, left, right = expert_call(x, shift(x, 1), shift(x, -1), wa, wb, ra, rb)]
    dot_general x6 -> x0, matrix products: 30.4 us -> none  [the longest x1 13 us: expert_apply(): jnp.dot(units, expert_down[0], preferred_element_type=jnp.float32)]
    all_to_all x0 -> x1, blocking collectives: none -> 28.5 us  [swap(): x = lax.all_to_all(x, 'expert', split_axis=0, concat_axis=0, tiled=True)]
    ppermute x0 -> x17, starting transfers between devices: none -> 28.2 us  [shift(): return lax.ppermute(x, 'dp', [(i, (i + k) % groups) for i in range(groups)])]
  transfers between devices with their start and end apart: 5 -> 23, of which waited for: 5 -> 8; matrix products, arithmetic and copies ran while one was open for 5% -> 9% of each run, Pallas kernels for 0% -> 11%
where the time goes in v1:
time: 297 us; the launch traced here: 292 us
  waiting for transfers between devices  96.9 us (33%)
  starting transfers between devices  93 us (31%)
  Pallas kernels  34.3 us (12%)
  local copies, waits for them, and re-layouts  29.8 us (10%)
  blocking collectives  28.5 us (10%)
  other arithmetic  8.05 us (3%)
    all_to_all x5, starting transfers between devices, swap(): x = lax.all_to_all(x, 'expert', split_axis=0, concat_axis=0, tiled=True)  61.3 us
    ppermute x17, waiting for transfers between devices, shift(): return lax.ppermute(x, 'dp', [(i, (i + k) % groups) for i in range(groups)])  48 us
    all_to_all x1, blocking collectives, swap(): x = lax.all_to_all(x, 'expert', split_axis=0, concat_axis=0, tiled=True)  28.5 us
    ppermute x17, starting transfers between devices, shift(): return lax.ppermute(x, 'dp', [(i, (i + k) % groups) for i in range(groups)])  28.2 us
    pallas_call x3, Pallas kernels, per_device(): own, left, right = expert_call(x, shift(x, 1), shift(x, -1), wa, wb, ra, rb)  24.6 us
    all_to_all x1, waiting for transfers between devices, per_device(): lax.all_to_all(partial.reshape(groups, block, width), 'dp', split_axis=0,...  24.5 us
    all_to_all x5, waiting for transfers between devices, swap(): x = lax.all_to_all(x, 'expert', split_axis=0, concat_axis=0, tiled=True)  24.4 us
    unnamed x45, local copies, waits for them, and re-layouts  11.5 us
  transfers between devices with their start and end apart: 23, of which 8 were waited for; matrix products, arithmetic and copies ran while one was open for 9% of the time, Pallas kernels for 11%

profile of v1, /device:TPU:1, one launch (start us, length us, event | category | flops | bytes accessed | tf_op | source)
XLA Modules:
  0.0 292.4 jit_solution(10459239599038600317)
XLA Ops:
  0.6 0.9 reshape_squeeze.7
  1.7 1.2 maximum_maximum_fusion.k0
  2.8 2.1 collective-permute-start
  5.0 1.4 collective-permute-start.1
  6.3 1.6 collective-permute-start.2
  8.0 2.3 slice_bitcast_fusion
  10.3 5.3 %fusion.6 = (bf16[1,176,1,2048]{3,2,1,0:T(2,128)(2,1)}, bf16[1,176,1,2048]{3,2,1,0:T(2,128)(2,1)S(1)}, bf16[1,176,1,2048]{3,2,1,0:T(2,128)(2,1)S(1)}, bf16[1,176,1,2048]{3,2,1,0:T(2,128)(2,1)}) fusion(bf16[1,352,2,2048]{3,2,1,0:T(2,128)(2,1)S(1)} %copy-done.18), kind=kLoop, calls=%fused_computation.30 | loop fusion | bytes 5767168 | tf_op jit(solution)/shard_map/slice | solution.py:277
  16.6 0.9 collective-permute-start.5
  17.5 1.4 copy.30
  28.0 1.0 maximum_maximum_fusion.1.kn
  29.0 1.6 copy-done.1
  30.6 1.0 copy-done.3
  31.6 0.9 copy-done.15
  33.4 5.1 %attend.1 = bf16[128,2048]{1,0:T(8,128)(2,1)} custom-call(bf16[128,512]{1,0:T(8,128)(2,1)S(1)} %bitcast.57, bf16[128,256]{1,0:T(8,128)(2,1)S(1)} %bitcast.58, bf16[4,128,512]{2,1,0:T(8,128)(2,1)S(1)} %copy-done.2, bf16[256,640]{1,0:T(8,128)(2,1)S(1)} %maximum_maximum_fusion.k0, bf16[256,640]{1,0:T(8,128)(2,1)} %collective-permute-done.k1, ...), custom_call_target="tpu_custom_call" | custom-call | tf_op jit(solution)/shard_map/attend/pallas_call | solution.py:283
  38.5 3.5 %all-to-all-start = ((bf16[4,32,2048]{2,1,0:T(8,128)(2,1)}), bf16[4,32,2048]{2,1,0:T(8,128)(2,1)S(1)}, u32[]{:S(2)}, u32[]{:S(2)}) async-start(bf16[4,32,2048]{2,1,0:T(8,128)(2,1)} %bitcast.7), calls=%async_computation | async-start | bytes 1048576 | tf_op jit(solution)/shard_map/all_to_all | solution.py:307
  42.0 3.8 %copy_bitcast_fusion = (bf16[176,2048]{1,0:T(8,128)(2,1)}, bf16[176,2048]{1,0:T(8,128)(2,1)}) fusion(bf16[1,176,1,2048]{3,2,1,0:T(2,128)(2,1)} %get-tuple-element.41, bf16[1,176,1,2048]{3,2,1,0:T(2,128)(2,1)} %get-tuple-element.38), kind=kLoop, calls=%fused_computation.5 | loop fusion | bytes 2883584 | tf_op jit(solution)/shard_map/squeeze | solution.py:277
  45.8 24.5 %all-to-all-done.partial = bf16[4,32,2048]{2,1,0:T(8,128)(2,1)S(1)} async-done(((bf16[4,32,2048]{2,1,0:T(8,128)(2,1)}), bf16[4,32,2048]{2,1,0:T(8,128)(2,1)S(1)}, u32[]{:S(2)}, u32[]{:S(2)}) %all-to-all-start) | async-done | bytes 524320 | tf_op jit(solution)/shard_map/all_to_all | solution.py:307
  70.3 1.0 copy-done.12
  71.3 1.5 pack.1
  75.1 14.2 %all-to-all-start.1 = ((bf16[64,8,512]{2,1,0:T(8,128)(2,1)}), bf16[64,8,512]{2,1,0:T(8,128)(2,1)}, u32[]{:S(2)}, u32[]{:S(2)}) async-start(bf16[64,8,512]{2,1,0:T(8,128)(2,1)} %bitcast.56), calls=%async_computation.1 | async-start | bytes 1048576 | tf_op jit(solution)/shard_map/all_to_all | solution.py:321
  89.4 3.2 %pad_maximum_fusion.1.wb = bf16[528,2048]{1,0:T(8,128)(2,1)} fusion(bf16[176,2048]{1,0:T(8,128)(2,1)} %get-tuple-element.42, bf16[176,2048]{1,0:T(8,128)(2,1)} %get-tuple-element.44, bf16[176,2048]{1,0:T(8,128)(2,1)} %get-tuple-element.45), kind=kLoop, calls=%fused_computation.1 | loop fusion | flops 6488064 | bytes 4325376 | tf_op jit(solution)/shard_map/concatenate | solution.py:276
  92.6 3.5 %collective-permute-start.6 = (bf16[528,2048]{1,0:T(8,128)(2,1)}, bf16[528,2048]{1,0:T(8,128)(2,1)}, u32[]{:S(2)}, u32[]{:S(2)}) collective-permute-start(bf16[528,2048]{1,0:T(8,128)(2,1)} %pad_maximum_fusion.1.wb), channel_id=1, source_target_pairs={{0,64},{64,128},{128,192},{192,0},{1,65},{65,129},{129,193},{193,1... | collective-permute-start | bytes 6488072 | tf_op jit(solution)/shard_map/ppermute | solution.py:236
  96.0 11.0 %all-to-all-done.1 = bf16[64,8,512]{2,1,0:T(8,128)(2,1)} async-done(((bf16[64,8,512]{2,1,0:T(8,128)(2,1)}), bf16[64,8,512]{2,1,0:T(8,128)(2,1)}, u32[]{:S(2)}, u32[]{:S(2)}) %all-to-all-start.1) | async-done | bytes 524320 | tf_op jit(solution)/shard_map/all_to_all | solution.py:321
  107.0 5.9 %all-to-all-start.3 = ((bf16[64,8,512]{2,1,0:T(8,128)(2,1)}), bf16[64,8,512]{2,1,0:T(8,128)(2,1)}, u32[]{:S(2)}, u32[]{:S(2)}) async-start(bf16[64,8,512]{2,1,0:T(8,128)(2,1)} %bitcast.22), calls=%async_computation.3 | async-start | bytes 1048576 | tf_op jit(solution)/shard_map/all_to_all | solution.py:321
  112.9 3.3 %collective-permute-start.3 = (bf16[512,512]{1,0:T(8,128)(2,1)}, bf16[512,512]{1,0:T(8,128)(2,1)}, u32[]{:S(2)}, u32[]{:S(2)}) collective-permute-start(bf16[512,512]{1,0:T(8,128)(2,1)} %bitcast.13.x0), channel_id=1, source_target_pairs={{0,64},{64,128},{128,192},{192,0},{1,65},{65,129},{129,193},{193,1... | collective-permute-start | bytes 1572872 | tf_op jit(solution)/shard_map/ppermute | solution.py:236
  116.3 0.9 collective-permute-start.4
  117.1 13.4 %all-to-all-done.3 = bf16[64,8,512]{2,1,0:T(8,128)(2,1)} async-done(((bf16[64,8,512]{2,1,0:T(8,128)(2,1)}), bf16[64,8,512]{2,1,0:T(8,128)(2,1)}, u32[]{:S(2)}, u32[]{:S(2)}) %all-to-all-start.3) | async-done | bytes 524320 | tf_op jit(solution)/shard_map/all_to_all | solution.py:321
  130.6 5.7 %all-to-all-start.5 = ((bf16[64,8,512]{2,1,0:T(8,128)(2,1)}), bf16[64,8,512]{2,1,0:T(8,128)(2,1)S(1)}, u32[]{:S(2)}, u32[]{:S(2)}) async-start(bf16[64,8,512]{2,1,0:T(8,128)(2,1)} %bitcast.55), calls=%async_computation.5 | async-start | bytes 1048576 | tf_op jit(solution)/shard_map/all_to_all | solution.py:321
  136.3 7.8 %collective-permute-done.6.rb = bf16[528,2048]{1,0:T(8,128)(2,1)} collective-permute-done((bf16[528,2048]{1,0:T(8,128)(2,1)}, bf16[528,2048]{1,0:T(8,128)(2,1)}, u32[]{:S(2)}, u32[]{:S(2)}) %collective-permute-start.6) | collective-permute-done | bytes 2162720 | tf_op jit(solution)/shard_map/ppermute | solution.py:236
  144.1 11.2 %collective-permute-done.3.xl = bf16[512,512]{1,0:T(8,128)(2,1)} collective-permute-done((bf16[512,512]{1,0:T(8,128)(2,1)}, bf16[512,512]{1,0:T(8,128)(2,1)}, u32[]{:S(2)}, u32[]{:S(2)}) %collective-permute-start.3) | collective-permute-done | bytes 524320 | tf_op jit(solution)/shard_map/ppermute | solution.py:236
  155.3 8.2 %experts.3 = (bf16[512,512]{1,0:T(8,128)(2,1)S(1)}, bf16[512,512]{1,0:T(8,128)(2,1)S(1)}, bf16[512,512]{1,0:T(8,128)(2,1)S(1)}) custom-call(bf16[512,512]{1,0:T(8,128)(2,1)} %bitcast.13.x0, bf16[512,512]{1,0:T(8,128)(2,1)} %collective-permute-done.3.xl, bf16[512,512]{1,0:T(8,128)(2,1)} %collective-permute-done.4.xr, ...), custom_call_target="tpu_custom_call" | custom-call | tf_op jit(solution)/shard_map/experts/pallas_call | solution.py:337
  164.0 2.3 collective-permute-start.7
  166.3 2.7 collective-permute-start.10
  169.0 8.2 %collective-permute-done.8 = bf16[512,512]{1,0:T(8,128)(2,1)S(1)} collective-permute-done((bf16[512,512]{1,0:T(8,128)(2,1)S(1)}, bf16[512,512]{1,0:T(8,128)(2,1)S(1)}, u32[]{:S(2)}, u32[]{:S(2)}) %collective-permute-start.8) | collective-permute-done | bytes 524320 | tf_op jit(solution)/shard_map/ppermute | solution.py:236
  177.2 1.0 fusion
  178.3 23.7 %all-to-all-start.2 = ((bf16[64,8,512]{2,1,0:T(8,128)(2,1)}), bf16[64,8,512]{2,1,0:T(8,128)(2,1)}, u32[]{:S(2)}, u32[]{:S(2)}) async-start(bf16[64,8,512]{2,1,0:T(8,128)(2,1)} %fusion), calls=%async_computation.2 | async-start | bytes 1048576 | tf_op jit(solution)/shard_map/all_to_all | solution.py:321
  202.0 8.3 %experts.4 = (bf16[512,512]{1,0:T(8,128)(2,1)S(1)}, bf16[512,512]{1,0:T(8,128)(2,1)S(1)}, bf16[512,512]{1,0:T(8,128)(2,1)S(1)}) custom-call(bf16[512,512]{1,0:T(8,128)(2,1)} %bitcast.23.x0, bf16[512,512]{1,0:T(8,128)(2,1)} %collective-permute-done.9.xl, bf16[512,512]{1,0:T(8,128)(2,1)} %collective-permute-done.10.xr, ...), custom_call_target="tpu_custom_call" | custom-call | tf_op jit(solution)/shard_map/experts/pallas_call | solution.py:337
  210.4 3.0 %collective-permute-start.11 = (bf16[512,512]{1,0:T(8,128)(2,1)S(1)}, bf16[512,512]{1,0:T(8,128)(2,1)S(1)}, u32[]{:S(2)}, u32[]{:S(2)}) collective-permute-start(bf16[512,512]{1,0:T(8,128)(2,1)S(1)} %get-tuple-element.30), channel_id=1, source_target_pairs={{0,192},{64,0},{128,64},{192,128},{1,193},{65,1},{129,65},{193,129... | collective-permute-start | bytes 1572872 | tf_op jit(solution)/shard_map/ppermute | solution.py:236
  213.4 2.7 collective-permute-start.14
  216.1 9.0 %collective-permute-done.12 = bf16[512,512]{1,0:T(8,128)(2,1)S(1)} collective-permute-done((bf16[512,512]{1,0:T(8,128)(2,1)S(1)}, bf16[512,512]{1,0:T(8,128)(2,1)S(1)}, u32[]{:S(2)}, u32[]{:S(2)}) %collective-permute-start.12) | collective-permute-done | bytes 524320 | tf_op jit(solution)/shard_map/ppermute | solution.py:236
  225.1 1.0 fusion.1
  226.1 11.7 %all-to-all-start.4 = ((bf16[64,8,512]{2,1,0:T(8,128)(2,1)}), bf16[64,8,512]{2,1,0:T(8,128)(2,1)}, u32[]{:S(2)}, u32[]{:S(2)}) async-start(bf16[64,8,512]{2,1,0:T(8,128)(2,1)} %fusion.1), calls=%async_computation.4 | async-start | bytes 1048576 | tf_op jit(solution)/shard_map/all_to_all | solution.py:321
  237.9 8.1 %experts.5 = (bf16[512,512]{1,0:T(8,128)(2,1)S(1)}, bf16[512,512]{1,0:T(8,128)(2,1)S(1)}, bf16[512,512]{1,0:T(8,128)(2,1)S(1)}) custom-call(bf16[512,512]{1,0:T(8,128)(2,1)S(1)} %bitcast.53, bf16[512,512]{1,0:T(8,128)(2,1)} %collective-permute-done.13.xl, bf16[512,512]{1,0:T(8,128)(2,1)} %collective-permute-done.14.xr, ...), custom_call_target="tpu_custom_call" | custom-call | tf_op jit(solution)/shard_map/experts/pallas_call | solution.py:337
  246.0 1.2 collective-permute-start.16
  247.2 2.0 collective-permute-start.15
  249.2 11.7 %collective-permute-done.16 = bf16[512,512]{1,0:T(8,128)(2,1)S(1)} collective-permute-done((bf16[512,512]{1,0:T(8,128)(2,1)S(1)}, bf16[512,512]{1,0:T(8,128)(2,1)S(1)}, u32[]{:S(2)}, u32[]{:S(2)}) %collective-permute-start.16) | collective-permute-done | bytes 524320 | tf_op jit(solution)/shard_map/ppermute | solution.py:236
  261.2 28.5 %all_to_all.35 = bf16[64,8,512]{2,1,0:T(8,128)(2,1)S(1)} all-to-all(bf16[64,8,512]{2,1,0:T(8,128)(2,1)S(1)} %fusion.2), channel_id=1, replica_groups=mesh['dp'=4,'expert'=64] {'expert'}, dimensions={0} | all-to-all | bytes 1048576 | tf_op jit(solution)/shard_map/all_to_all | solution.py:321
  289.7 2.5 combine.1
  (79 shorter events, 13.4 us)
Async XLA Ops:
  0.6 19.5 %copy-start = (bf16[1,128,2048]{2,1,0:T(8,128)(2,1)S(1)}, bf16[1,128,2048]{2,1,0:T(8,128)(2,1)}, u32[]{:S(2)}) copy-start(bf16[1,128,2048]{2,1,0:T(8,128)(2,1)} %param.26) | copy-start | bytes 1572868
  1.6 8.7 %copy-start.18 = (bf16[1,352,2,2048]{3,2,1,0:T(2,128)(2,1)S(1)}, bf16[1,352,2,2048]{3,2,1,0:T(2,128)(2,1)}, u32[]{:S(2)}) copy-start(bf16[1,352,2,2048]{3,2,1,0:T(2,128)(2,1)} %param.31) | copy-start | bytes 8650756
  2.8 26.1 %collective-permute-start = (bf16[256,640]{1,0:T(8,128)(2,1)S(1)}, bf16[256,640]{1,0:T(8,128)(2,1)}, u32[]{:S(2)}, u32[]{:S(2)}) collective-permute-start(bf16[256,640]{1,0:T(8,128)(2,1)S(1)} %maximum_maximum_fusion.k0), channel_id=1, source_target_pairs={{0,64},{64,128},{128,192},{192,0},{1,65},{65,129},{129,193},{193,1... | collective-permute-start | bytes 983048 | tf_op jit(solution)/shard_map/ppermute | solution.py:236
  5.0 24.0 %collective-permute-start.1 = (bf16[256,640]{1,0:T(8,128)(2,1)S(1)}, bf16[256,640]{1,0:T(8,128)(2,1)}, u32[]{:S(2)}, u32[]{:S(2)}) collective-permute-start(bf16[256,640]{1,0:T(8,128)(2,1)S(1)} %maximum_maximum_fusion.k0), channel_id=1, source_target_pairs={{0,192},{64,0},{128,64},{192,128},{1,193},{65,1},{129,65},{193,129... | collective-permute-start | bytes 983048 | tf_op jit(solution)/shard_map/ppermute | solution.py:236
  6.3 22.7 %collective-permute-start.2 = (bf16[256,640]{1,0:T(8,128)(2,1)S(1)}, bf16[256,640]{1,0:T(8,128)(2,1)}, u32[]{:S(2)}, u32[]{:S(2)}) collective-permute-start(bf16[256,640]{1,0:T(8,128)(2,1)S(1)} %maximum_maximum_fusion.k0), channel_id=1, source_target_pairs={{0,128},{64,192},{128,0},{192,64},{1,129},{65,193},{129,1},{193,65... | collective-permute-start | bytes 983048 | tf_op jit(solution)/shard_map/ppermute | solution.py:236
  16.4 3.2 %copy-start.20 = (s32[4]{0:T(128)S(1)}, s32[4]{0:T(128)}, u32[]{:S(2)}) copy-start(s32[4]{0:T(128)} %constant.32.clone) | copy-start | bytes 52
  16.4 3.4 %copy-start.19 = (s32[1,16]{1,0:T(1,128)S(1)}, s32[1,16]{1,0:T(1,128)}, u32[]{:S(2)}) copy-start(s32[1,16]{1,0:T(1,128)} %param.24) | copy-start | bytes 196
  16.4 12.6 %copy-start.2 = (bf16[4,128,512]{2,1,0:T(8,128)(2,1)S(1)}, bf16[4,128,512]{2,1,0:T(8,128)(2,1)}, u32[]{:S(2)}) copy-start(bf16[4,128,512]{2,1,0:T(8,128)(2,1)} %ku.1) | copy-start | bytes 1572868
  16.6 119.7 %collective-permute-start.5 = (bf16[528,2048]{1,0:T(8,128)(2,1)S(1)}, bf16[528,2048]{1,0:T(8,128)(2,1)}, u32[]{:S(2)}, u32[]{:S(2)}) collective-permute-start(bf16[528,2048]{1,0:T(8,128)(2,1)S(1)} %pad_maximum_fusion.wa), channel_id=1, source_target_pairs={{0,192},{64,0},{128,64},{192,128},{1,193},{65,1},{129,65},{193,129... | collective-permute-start | bytes 6488072 | tf_op jit(solution)/shard_map/ppermute | solution.py:236
  25.7 0.8 copy-start.7
  26.5 0.7 copy-start.9
  27.2 0.8 copy-start.11
  29.0 1.6 copy-start.1
  30.6 1.0 copy-start.3
  31.6 0.9 copy-start.15
  32.5 0.8 copy-start.16
  38.5 31.8 %all-to-all-start = ((bf16[4,32,2048]{2,1,0:T(8,128)(2,1)}), bf16[4,32,2048]{2,1,0:T(8,128)(2,1)S(1)}, u32[]{:S(2)}, u32[]{:S(2)}) async-start(bf16[4,32,2048]{2,1,0:T(8,128)(2,1)} %bitcast.7), calls=%async_computation | async-start | bytes 1048576 | tf_op jit(solution)/shard_map/all_to_all | solution.py:307
  42.0 28.3 %copy-start.6 = (bf16[32,2048]{1,0:T(8,128)(2,1)S(1)}, bf16[32,2048]{1,0:T(8,128)(2,1)}, u32[]{:S(2)}) copy-start(bf16[32,2048]{1,0:T(8,128)(2,1)} %dynamic-slice_bitcast_fusion.residual) | copy-start | bytes 393220
  42.0 28.3 %copy-start.17 = (f32[2048]{0:T(1024)S(1)}, f32[2048]{0:T(1024)}, u32[]{:S(2)}) copy-start(f32[2048]{0:T(1024)} %param.30) | copy-start | bytes 24580
  70.3 1.0 copy-start.12
  72.8 0.8 copy-start.4
  73.6 0.8 copy-start.5
  74.4 0.7 copy-start.13
  75.1 31.9 %all-to-all-start.1 = ((bf16[64,8,512]{2,1,0:T(8,128)(2,1)}), bf16[64,8,512]{2,1,0:T(8,128)(2,1)}, u32[]{:S(2)}, u32[]{:S(2)}) async-start(bf16[64,8,512]{2,1,0:T(8,128)(2,1)} %bitcast.56), calls=%async_computation.1 | async-start | bytes 1048576 | tf_op jit(solution)/shard_map/all_to_all | solution.py:321
  92.6 51.5 %collective-permute-start.6 = (bf16[528,2048]{1,0:T(8,128)(2,1)}, bf16[528,2048]{1,0:T(8,128)(2,1)}, u32[]{:S(2)}, u32[]{:S(2)}) collective-permute-start(bf16[528,2048]{1,0:T(8,128)(2,1)} %pad_maximum_fusion.1.wb), channel_id=1, source_target_pairs={{0,64},{64,128},{128,192},{192,0},{1,65},{65,129},{129,193},{193,1... | collective-permute-start | bytes 6488072 | tf_op jit(solution)/shard_map/ppermute | solution.py:236
  107.0 23.6 %all-to-all-start.3 = ((bf16[64,8,512]{2,1,0:T(8,128)(2,1)}), bf16[64,8,512]{2,1,0:T(8,128)(2,1)}, u32[]{:S(2)}, u32[]{:S(2)}) async-start(bf16[64,8,512]{2,1,0:T(8,128)(2,1)} %bitcast.22), calls=%async_computation.3 | async-start | bytes 1048576 | tf_op jit(solution)/shard_map/all_to_all | solution.py:321
  112.9 42.4 %collective-permute-start.3 = (bf16[512,512]{1,0:T(8,128)(2,1)}, bf16[512,512]{1,0:T(8,128)(2,1)}, u32[]{:S(2)}, u32[]{:S(2)}) collective-permute-start(bf16[512,512]{1,0:T(8,128)(2,1)} %bitcast.13.x0), channel_id=1, source_target_pairs={{0,64},{64,128},{128,192},{192,0},{1,65},{65,129},{129,193},{193,1... | collective-permute-start | bytes 1572872 | tf_op jit(solution)/shard_map/ppermute | solution.py:236
  116.3 39.1 %collective-permute-start.4 = (bf16[512,512]{1,0:T(8,128)(2,1)}, bf16[512,512]{1,0:T(8,128)(2,1)}, u32[]{:S(2)}, u32[]{:S(2)}) collective-permute-start(bf16[512,512]{1,0:T(8,128)(2,1)} %bitcast.13.x0), channel_id=1, source_target_pairs={{0,192},{64,0},{128,64},{192,128},{1,193},{65,1},{129,65},{193,129... | collective-permute-start | bytes 1572872 | tf_op jit(solution)/shard_map/ppermute | solution.py:236
  130.6 47.7 %all-to-all-start.5 = ((bf16[64,8,512]{2,1,0:T(8,128)(2,1)}), bf16[64,8,512]{2,1,0:T(8,128)(2,1)S(1)}, u32[]{:S(2)}, u32[]{:S(2)}) async-start(bf16[64,8,512]{2,1,0:T(8,128)(2,1)} %bitcast.55), calls=%async_computation.5 | async-start | bytes 1048576 | tf_op jit(solution)/shard_map/all_to_all | solution.py:321
  163.6 13.6 %collective-permute-start.8 = (bf16[512,512]{1,0:T(8,128)(2,1)S(1)}, bf16[512,512]{1,0:T(8,128)(2,1)S(1)}, u32[]{:S(2)}, u32[]{:S(2)}) collective-permute-start(bf16[512,512]{1,0:T(8,128)(2,1)S(1)} %get-tuple-element.27), channel_id=1, source_target_pairs={{0,64},{64,128},{128,192},{192,0},{1,65},{65,129},{129,193},{193,1... | collective-permute-start | bytes 1572872 | tf_op jit(solution)/shard_map/ppermute | solution.py:236
  164.0 13.2 %collective-permute-start.7 = (bf16[512,512]{1,0:T(8,128)(2,1)S(1)}, bf16[512,512]{1,0:T(8,128)(2,1)S(1)}, u32[]{:S(2)}, u32[]{:S(2)}) collective-permute-start(bf16[512,512]{1,0:T(8,128)(2,1)S(1)} %get-tuple-element.26), channel_id=1, source_target_pairs={{0,192},{64,0},{128,64},{192,128},{1,193},{65,1},{129,65},{193,129... | collective-permute-start | bytes 1572872 | tf_op jit(solution)/shard_map/ppermute | solution.py:236
  166.3 35.7 %collective-permute-start.9 = (bf16[512,512]{1,0:T(8,128)(2,1)}, bf16[512,512]{1,0:T(8,128)(2,1)}, u32[]{:S(2)}, u32[]{:S(2)}) collective-permute-start(bf16[512,512]{1,0:T(8,128)(2,1)} %bitcast.23.x0), channel_id=1, source_target_pairs={{0,64},{64,128},{128,192},{192,0},{1,65},{65,129},{129,193},{193,1... | collective-permute-start | bytes 1572872 | tf_op jit(solution)/shard_map/ppermute | solution.py:236
  166.3 35.7 %collective-permute-start.10 = (bf16[512,512]{1,0:T(8,128)(2,1)}, bf16[512,512]{1,0:T(8,128)(2,1)}, u32[]{:S(2)}, u32[]{:S(2)}) collective-permute-start(bf16[512,512]{1,0:T(8,128)(2,1)} %bitcast.23.x0), channel_id=1, source_target_pairs={{0,192},{64,0},{128,64},{192,128},{1,193},{65,1},{129,65},{193,129... | collective-permute-start | bytes 1572872 | tf_op jit(solution)/shard_map/ppermute | solution.py:236
  178.3 47.8 %all-to-all-start.2 = ((bf16[64,8,512]{2,1,0:T(8,128)(2,1)}), bf16[64,8,512]{2,1,0:T(8,128)(2,1)}, u32[]{:S(2)}, u32[]{:S(2)}) async-start(bf16[64,8,512]{2,1,0:T(8,128)(2,1)} %fusion), calls=%async_computation.2 | async-start | bytes 1048576 | tf_op jit(solution)/shard_map/all_to_all | solution.py:321
  210.3 14.8 %collective-permute-start.12 = (bf16[512,512]{1,0:T(8,128)(2,1)S(1)}, bf16[512,512]{1,0:T(8,128)(2,1)S(1)}, u32[]{:S(2)}, u32[]{:S(2)}) collective-permute-start(bf16[512,512]{1,0:T(8,128)(2,1)S(1)} %get-tuple-element.31), channel_id=1, source_target_pairs={{0,64},{64,128},{128,192},{192,0},{1,65},{65,129},{129,193},{193,1... | collective-permute-start | bytes 1572872 | tf_op jit(solution)/shard_map/ppermute | solution.py:236
  210.4 14.7 %collective-permute-start.11 = (bf16[512,512]{1,0:T(8,128)(2,1)S(1)}, bf16[512,512]{1,0:T(8,128)(2,1)S(1)}, u32[]{:S(2)}, u32[]{:S(2)}) collective-permute-start(bf16[512,512]{1,0:T(8,128)(2,1)S(1)} %get-tuple-element.30), channel_id=1, source_target_pairs={{0,192},{64,0},{128,64},{192,128},{1,193},{65,1},{129,65},{193,129... | collective-permute-start | bytes 1572872 | tf_op jit(solution)/shard_map/ppermute | solution.py:236
  213.4 24.4 %collective-permute-start.13 = (bf16[512,512]{1,0:T(8,128)(2,1)S(1)}, bf16[512,512]{1,0:T(8,128)(2,1)}, u32[]{:S(2)}, u32[]{:S(2)}) collective-permute-start(bf16[512,512]{1,0:T(8,128)(2,1)S(1)} %bitcast.51), channel_id=1, source_target_pairs={{0,64},{64,128},{128,192},{192,0},{1,65},{65,129},{129,193},{193,1... | collective-permute-start | bytes 1572872 | tf_op jit(solution)/shard_map/ppermute | solution.py:236
  213.4 24.4 %collective-permute-start.14 = (bf16[512,512]{1,0:T(8,128)(2,1)S(1)}, bf16[512,512]{1,0:T(8,128)(2,1)}, u32[]{:S(2)}, u32[]{:S(2)}) collective-permute-start(bf16[512,512]{1,0:T(8,128)(2,1)S(1)} %bitcast.52), channel_id=1, source_target_pairs={{0,192},{64,0},{128,64},{192,128},{1,193},{65,1},{129,65},{193,129... | collective-permute-start | bytes 1572872 | tf_op jit(solution)/shard_map/ppermute | solution.py:236
  226.1 35.1 %all-to-all-start.4 = ((bf16[64,8,512]{2,1,0:T(8,128)(2,1)}), bf16[64,8,512]{2,1,0:T(8,128)(2,1)}, u32[]{:S(2)}, u32[]{:S(2)}) async-start(bf16[64,8,512]{2,1,0:T(8,128)(2,1)} %fusion.1), calls=%async_computation.4 | async-start | bytes 1048576 | tf_op jit(solution)/shard_map/all_to_all | solution.py:321
  246.0 43.7 %copy-start.8 = (bf16[3,512,128]{2,1,0:T(8,128)(2,1)S(1)}, bf16[3,512,128]{2,1,0:T(8,128)(2,1)}, u32[]{:S(2)}) copy-start(bf16[3,512,128]{2,1,0:T(8,128)(2,1)} %copy-done.7) | copy-start | bytes 1179652
  246.0 43.7 %copy-start.10 = (bf16[3,512,128]{2,1,0:T(8,128)(2,1)S(1)}, bf16[3,512,128]{2,1,0:T(8,128)(2,1)}, u32[]{:S(2)}) copy-start(bf16[3,512,128]{2,1,0:T(8,128)(2,1)} %copy-done.9) | copy-start | bytes 1179652
  246.0 43.7 %copy-start.14 = (f32[32,2048]{1,0:T(8,128)S(1)}, f32[32,2048]{1,0:T(8,128)}, u32[]{:S(2)}) copy-start(f32[32,2048]{1,0:T(8,128)} %copy-done.13) | copy-start | bytes 786436
  246.0 15.0 %collective-permute-start.16 = (bf16[512,512]{1,0:T(8,128)(2,1)S(1)}, bf16[512,512]{1,0:T(8,128)(2,1)S(1)}, u32[]{:S(2)}, u32[]{:S(2)}) collective-permute-start(bf16[512,512]{1,0:T(8,128)(2,1)S(1)} %get-tuple-element.35), channel_id=1, source_target_pairs={{0,64},{64,128},{128,192},{192,0},{1,65},{65,129},{129,193},{193,1... | collective-permute-start | bytes 1572872 | tf_op jit(solution)/shard_map/ppermute | solution.py:236
  247.2 13.7 %collective-permute-start.15 = (bf16[512,512]{1,0:T(8,128)(2,1)S(1)}, bf16[512,512]{1,0:T(8,128)(2,1)S(1)}, u32[]{:S(2)}, u32[]{:S(2)}) collective-permute-start(bf16[512,512]{1,0:T(8,128)(2,1)S(1)} %get-tuple-element.34), channel_id=1, source_target_pairs={{0,192},{64,0},{128,64},{192,128},{1,193},{65,1},{129,65},{193,129... | collective-permute-start | bytes 1572872 | tf_op jit(solution)/shard_map/ppermute | solution.py:236
